TPU v7x, 512 devices: a whole 4x4x16 slice. The times are simulated.
512 devices in a mesh: seq: 128 (over z, x, core), head: 4 (over y).
Axes of the slice: x: 4, y: 4, z: 16, core: 2. Of those that a mesh axis runs over, the one named last changes fastest.
Arguments:
- queries: bfloat16 [32768, 512], P('seq', 'head'), may hold values from -16 to 16
- keys: bfloat16 [32768, 512], P('seq', 'head'), may hold values from -16 to 16
- values: bfloat16 [32768, 512], P('seq', 'head'), may hold values from -16 to 16
- out_weight: bfloat16 [512, 512], replicated, may hold values from -0.5 to 0.5
Outputs:
- mixed: bfloat16 [32768, 512], P(('seq', 'head'))
All inputs are finite; a program needn't handle non-finite values.
Results may differ from a plain program's by a relative error of at most 0.00185.
The roundings to bfloat16 on the way count: a program that leaves them out, or rounds other values in their place, can miss the bound.
Values may be sent and summed in bfloat16 or wider, within the bound.
A program may use at most 128 MiB of HBM per device.

v0:
```python
import math
import jax
import jax.numpy as jnp
from jax import lax
from jax.sharding import PartitionSpec as P

HD = 64
LEAF = 128


def extended_2(cells, sides, width):
    for axis, dim in sides:
        count = lax.axis_size(axis)
        ends = count - 1
        head = lax.slice_in_dim(cells, 0, width, axis=dim)
        tail = lax.slice_in_dim(cells, cells.shape[dim] - width, cells.shape[dim], axis=dim)
        cells = jnp.concatenate(
            [
                lax.ppermute(tail, axis, [(i, (i + 1) % count) for i in range(ends)]),
                cells,
                lax.ppermute(head, axis, [((i + 1) % count, i) for i in range(ends)]),
            ],
            axis=dim,
        )
    return cells


def as_sent(x):

    def short(part):
        return part.astype(jnp.bfloat16) if part.dtype == jnp.float32 else part

    return jax.tree.map(short, x)


def average_pairs(stacked):
    widened = stacked.astype(jnp.float32).reshape(2, stacked.shape[1] // 2, 2, stacked.shape[2])
    return (0.5 * (widened[:, :, 0] + widened[:, :, 1])).astype(jnp.bfloat16)


def near_set(leaf, extended, seq_index, blocks_dev, seq_size):
    positions = jnp.arange(LEAF, dtype=jnp.int32)
    upper_half = positions >= LEAF // 2
    global_leaf = seq_index * blocks_dev + leaf
    all_blocks = seq_size * blocks_dev
    key_parts = [lax.dynamic_slice_in_dim(extended[0], leaf * LEAF, 3 * LEAF, 1)]
    neighbour = global_leaf - 1 + jnp.arange(3 * LEAF, dtype=jnp.int32) // LEAF
    valid_parts = [(neighbour >= 0) & (neighbour < all_blocks)]
    local_block = leaf >> 1
    global_block = global_leaf >> 1
    parity = global_leaf >> 0 & 1
    level_blocks = all_blocks >> 1
    key_parts.append(lax.dynamic_slice_in_dim(extended[1], local_block * LEAF, LEAF, 1))
    key_parts.append(lax.dynamic_slice_in_dim(extended[1], (local_block + 2) * LEAF, LEAF, 1))
    valid_parts.append((global_block >= 1) & jnp.logical_not(upper_half & (parity == 0)))
    valid_parts.append(
        (global_block + 1 < level_blocks)
        & jnp.logical_not(jnp.logical_not(upper_half) & (parity == 1))
    )
    return (jnp.concatenate(key_parts, axis=1), jnp.concatenate(valid_parts, axis=0))


def shards(queries, keys, values, out_weight):
    tok_count = queries.shape[0]
    width = queries.shape[1]
    seq_size = lax.axis_size("seq")
    seq_index = lax.axis_index("seq")
    blocks_dev = tok_count // LEAF
    near_count = blocks_dev.bit_length() - 1
    far_count = max(0, seq_size.bit_length() - 2)
    scale = 1.0 / math.sqrt(HD)
    positions = jnp.arange(LEAF, dtype=jnp.int32)
    upper_half = positions >= LEAF // 2
    local = [jnp.stack([keys, values], axis=0)]
    local.append(average_pairs(local[-1]))
    extended = [extended_2(stacked, (("seq", 1),), LEAF) for stacked in local]
    own_block = local[near_count]
    far_pairs = []
    far_valid = []
    everything = lax.all_gather(own_block, "seq", axis=1, tiled=True)
    for level_far in range(1, far_count + 1):
        everything = average_pairs(everything)
        group = seq_index >> level_far
        padded = jnp.pad(everything, ((0, 0), (LEAF, LEAF), (0, 0)))
        lower = lax.dynamic_slice_in_dim(padded, group * LEAF, LEAF, 1)
        upper = lax.dynamic_slice_in_dim(padded, (group + 2) * LEAF, LEAF, 1)
        far_pairs.append(jnp.concatenate([lower, upper], axis=1))
    for level_far in range(1, far_count + 1):
        group = seq_index >> level_far
        parity = seq_index >> level_far - 1 & 1
        far_valid.append((group >= 1) & jnp.logical_not(upper_half & (parity == 0)))
        far_valid.append(
            (group + 1 < seq_size >> level_far)
            & jnp.logical_not(jnp.logical_not(upper_half) & (parity == 1))
        )
    far_keys = jnp.concatenate(far_pairs, axis=1)
    far_mask = jnp.concatenate(far_valid, axis=0)
    leaves_step = min(blocks_dev, max(1, 512 // LEAF))
    step_count = blocks_dev // leaves_step

    def attend(step):
        leaves = step * leaves_step + jnp.arange(leaves_step, dtype=jnp.int32)
        near_keys, near_mask = jax.vmap(
            lambda leaf: near_set(leaf, extended, seq_index, blocks_dev, seq_size)
        )(leaves)
        query_block = queries.reshape(leaves_step, LEAF, width)
        head_outputs = []
        for head_number in range(width // HD):
            low_col = head_number * HD
            high_col = low_col + HD
            near_scores = (
                jnp.einsum(
                    "nhs,nos->nho",
                    query_block[:, :, low_col:high_col],
                    near_keys[:, 0, :, low_col:high_col],
                    preferred_element_type=jnp.float32,
                )
                * scale
            )
            near_scores = jnp.where(near_mask[:, None, :], near_scores, -jnp.inf)
            peak = jnp.max(near_scores, axis=-1, keepdims=True)
            far_scores = (
                jnp.einsum(
                    "qs,os->qo",
                    queries[:, low_col:high_col],
                    far_keys[0, :, low_col:high_col],
                    preferred_element_type=jnp.float32,
                )
                * scale
            )
            far_scores = far_scores.reshape(leaves_step, LEAF, far_scores.shape[-1])
            far_scores = jnp.where(far_mask[None, None, :], far_scores, -jnp.inf)
            peak = jnp.maximum(peak, jnp.max(far_scores, axis=-1, keepdims=True))
            near_weights = jnp.exp(near_scores - peak)
            total = jnp.sum(near_weights, axis=-1)
            numer = jnp.einsum(
                "fkm,fmp->fkp",
                near_weights.astype(jnp.bfloat16),
                near_keys[:, 1, :, low_col:high_col],
                preferred_element_type=jnp.float32,
            )
            far_weights = jnp.exp(far_scores - peak)
            total = total + jnp.sum(far_weights, axis=-1)
            far_rounded = far_weights.astype(jnp.bfloat16).reshape(
                leaves_step * LEAF, far_weights.shape[-1]
            )
            far_numer = jnp.dot(
                far_rounded, far_keys[1, :, low_col:high_col], preferred_element_type=jnp.float32
            )
            numer = numer + far_numer.reshape(leaves_step, LEAF, HD)
            head_outputs.append((numer / total[..., None]).astype(jnp.bfloat16))
        return jnp.concatenate(head_outputs, axis=-1).reshape(leaves_step * LEAF, width)

    attended = lax.map(attend, jnp.arange(step_count, dtype=jnp.int32)).reshape(tok_count, width)
    gathered_rows = lax.all_to_all(
        as_sent(attended), "head", split_axis=0, concat_axis=1, tiled=True
    ).astype(attended.dtype)
    return jnp.dot(gathered_rows, out_weight, preferred_element_type=jnp.float32).astype(
        jnp.bfloat16
    )


def solution(mesh):
    in_specs = (P("seq", "head"), P("seq", "head"), P("seq", "head"), P())
    out_specs = P(("seq", "head"), None)
    return jax.shard_map(shards, mesh=mesh, in_specs=in_specs, out_specs=out_specs, check_vma=False)
```

profile of v0, /device:TPU:32, one launch (start us, length us, event | category | flops | bytes accessed | tf_op | source)
XLA Modules:
  0.0 354.0 jit_solution(11749175016474953703)
XLA Ops:
  6.5 1.0 copy.43
  7.5 0.9 copy.44
  9.6 1.9 collective-permute-start.2
  11.6 5.8 %collective-permute-start.3 = (bf16[2,128,128]{2,0,1:T(2,128)(2,1)S(1)}, bf16[2,128,128]{2,0,1:T(2,128)(2,1)S(1)}, u32[]{:S(2)}, u32[]{:S(2)}) collective-permute-start(bf16[2,128,128]{2,0,1:T(2,128)(2,1)S(1)} %fusion.76), channel_id=1, source_target_pairs={{4,0},{8,4},{12,8},{16,12},{20,16},{24,20},{28,24},{32,28},{36,32}... | collective-permute-start | bytes 196616 | tf_op jit(solution)/shard_map/ppermute | solution.py:21
  17.3 0.9 copy.41
  18.3 0.9 copy.42
  19.5 1.9 collective-permute-start
  21.4 5.8 %collective-permute-start.1 = (bf16[2,128,128]{2,0,1:T(2,128)(2,1)S(1)}, bf16[2,128,128]{2,0,1:T(2,128)(2,1)S(1)}, u32[]{:S(2)}, u32[]{:S(2)}) collective-permute-start(bf16[2,128,128]{2,0,1:T(2,128)(2,1)S(1)} %get-tuple-element.46), channel_id=1, source_target_pairs={{4,0},{8,4},{12,8},{16,12},{20,16},{24,20},{28,24},{32,28},{36,32}... | collective-permute-start | bytes 196616 | tf_op jit(solution)/shard_map/ppermute | solution.py:21
  31.0 0.8 gather_fusion.1
  32.0 0.8 gather_fusion.2
  33.4 1.3 gather_fusion
  35.2 1.2 fusion.70
  36.4 1.2 fusion.68
  37.7 124.1 %all-gather.3.cloned.1.call-done = bf16[2,16384,1,128]{3,0,2,1:T(2,128)(2,1)} async-done(((bf16[2,128,1,128]{3,0,2,1:T(2,128)(2,1)}), bf16[2,16384,1,128]{3,0,2,1:T(2,128)(2,1)}) %all-gather.3.cloned.1.call-update) | async-done | bytes 8388624 | tf_op jit(solution)/shard_map/all_gather | solution.py:80
  161.8 5.1 %copy.50 = bf16[2,16384,1,128]{3,1,0,2:T(8,128)(2,1)S(1)} copy(bf16[2,16384,1,128]{3,0,2,1:T(2,128)(2,1)} %all-gather.3.cloned.1.call-done) | data formatting | bytes 16777216 | tf_op jit(solution)/shard_map/all_gather | solution.py:80
  166.8 13.0 %fusion.63 = (f32[2,8192,1,128]{3,2,1,0:T(1,128)}, f32[2,8192,1,128]{3,2,1,0:T(1,128)}) fusion(bf16[2,8192,2,128]{3,2,1,0:T(2,128)(2,1)S(1)} %bitcast.97), kind=kLoop, calls=%fused_computation.146 | loop fusion | bytes 33554432 | tf_op jit(solution)/shard_map/slice | solution.py:38
  179.8 18.0 %copy.76 = f32[2,8192,1,128]{1,3,0,2:T(8,128)} copy(f32[2,8192,1,128]{3,2,1,0:T(1,128)} %get-tuple-element.22) | data formatting | bytes 16777216
  197.8 18.0 %copy.77 = f32[2,8192,1,128]{1,3,0,2:T(8,128)} copy(f32[2,8192,1,128]{3,2,1,0:T(1,128)} %get-tuple-element.21) | data formatting | bytes 16777216
  215.8 9.4 %multiply_convert_fusion = bf16[2,8192,1,128]{1,3,0,2:T(8,128)(2,1)} fusion(f32[2,8192,1,128]{1,3,0,2:T(8,128)} %copy.76, f32[2,8192,1,128]{1,3,0,2:T(8,128)} %copy.77), kind=kLoop, calls=%fused_computation.3 | loop fusion | flops 6291456 | bytes 20971520 | tf_op jit(solution)/shard_map/convert_element_type | solution.py:38
  225.2 7.0 %copy.53 = f32[2,8192,1,128]{3,1,0,2:T(8,128)} copy(bf16[2,8192,1,128]{1,3,0,2:T(8,128)(2,1)} %multiply_convert_fusion) | data formatting | bytes 12582912 | tf_op jit(solution)/shard_map/convert_element_type | solution.py:37
  232.3 11.5 %fusion.62 = (f32[2,4096,1,128]{3,2,1,0:T(1,128)}, f32[2,4096,1,128]{3,2,1,0:T(1,128)}) fusion(f32[2,4096,2,128]{3,2,1,0:T(2,128)} %bitcast.102), kind=kLoop, calls=%fused_computation.145 | loop fusion | bytes 16777216 | tf_op jit(solution)/shard_map/slice | solution.py:38
  243.8 10.2 %copy.78 = f32[2,4096,1,128]{1,3,0,2:T(8,128)} copy(f32[2,4096,1,128]{3,2,1,0:T(1,128)} %get-tuple-element.20) | data formatting | bytes 8388608
  254.0 10.2 %copy.79 = f32[2,4096,1,128]{1,3,0,2:T(8,128)} copy(f32[2,4096,1,128]{3,2,1,0:T(1,128)} %get-tuple-element.19) | data formatting | bytes 8388608
  264.1 4.3 %multiply_convert_fusion.1 = bf16[2,4096,1,128]{1,3,0,2:T(8,128)(2,1)S(1)} fusion(f32[2,4096,1,128]{1,3,0,2:T(8,128)} %copy.78, f32[2,4096,1,128]{1,3,0,2:T(8,128)} %copy.79), kind=kLoop, calls=%fused_computation.4 | loop fusion | flops 3145728 | bytes 10485760 | tf_op jit(solution)/shard_map/convert_element_type | solution.py:38
  268.5 2.9 copy.56
  271.4 7.9 %fusion.64 = (f32[2,2048,1,128]{3,2,1,0:T(1,128)}, f32[2,2048,1,128]{3,2,1,0:T(1,128)}) fusion(f32[2,2048,2,128]{3,2,1,0:T(2,128)} %bitcast.105), kind=kLoop, calls=%fused_computation.147 | loop fusion | bytes 8388608 | tf_op jit(solution)/shard_map/slice | solution.py:38
  279.3 6.1 %copy.80 = f32[2,2048,1,128]{1,3,0,2:T(8,128)} copy(f32[2,2048,1,128]{3,2,1,0:T(1,128)} %get-tuple-element.32) | data formatting | bytes 4194304
  285.4 6.1 %copy.81 = f32[2,2048,1,128]{1,3,0,2:T(8,128)} copy(f32[2,2048,1,128]{3,2,1,0:T(1,128)} %get-tuple-element.23) | data formatting | bytes 4194304
  291.5 3.6 %multiply_convert_fusion.2 = bf16[2,2048,1,128]{1,3,0,2:T(8,128)(2,1)} fusion(f32[2,2048,1,128]{1,3,0,2:T(8,128)} %copy.80, f32[2,2048,1,128]{1,3,0,2:T(8,128)} %copy.81), kind=kLoop, calls=%fused_computation.11 | loop fusion | flops 1572864 | bytes 5242880 | tf_op jit(solution)/shard_map/convert_element_type | solution.py:38
  295.1 2.6 copy.59
  297.7 5.4 %fusion.65 = (f32[2,1024,1,128]{3,2,1,0:T(1,128)}, f32[2,1024,1,128]{3,2,1,0:T(1,128)}) fusion(f32[2,1024,2,128]{3,2,1,0:T(2,128)} %bitcast.108), kind=kLoop, calls=%fused_computation.148 | loop fusion | bytes 4194304 | tf_op jit(solution)/shard_map/slice | solution.py:38
  303.1 3.6 %copy.82 = f32[2,1024,1,128]{1,3,0,2:T(8,128)} copy(f32[2,1024,1,128]{3,2,1,0:T(1,128)} %get-tuple-element.36) | data formatting | bytes 2097152
  306.7 3.6 %copy.83 = f32[2,1024,1,128]{1,3,0,2:T(8,128)} copy(f32[2,1024,1,128]{3,2,1,0:T(1,128)} %get-tuple-element.34) | data formatting | bytes 2097152
  310.3 1.8 multiply_convert_fusion.3
  312.1 1.2 copy.62
  313.3 3.5 fusion.66
  316.8 1.9 copy.84
  318.7 1.9 copy.85
  320.6 1.3 multiply_convert_fusion.4
  321.9 0.9 copy.65
  322.9 2.5 fusion.67
  325.4 1.8 copy.86
  327.1 1.8 copy.87
  328.9 1.0 fusion.27
  329.9 1.2 copy-done.1
  331.3 1.1 copy-done.2
  336.6 9.7 %all_to_all.19 = bf16[4,64,128]{2,1,0:T(8,128)(2,1)S(1)} all-to-all(bf16[4,64,128]{2,1,0:T(8,128)(2,1)S(1)} %bitcast.121), channel_id=1, replica_groups=mesh['seq'=128,'head'=4] {'head'}, dimensions={0} | all-to-all | bytes 131072 | tf_op jit(solution)/shard_map/all_to_all | solution.py:155
  346.3 0.8 convolution_convert_fusion
  (101 shorter events, 10.4 us)
Async XLA Ops:
  6.5 339.8 %copy-start = (bf16[512,512]{1,0:T(8,128)(2,1)S(1)}, bf16[512,512]{1,0:T(8,128)(2,1)}, u32[]{:S(2)}) copy-start(bf16[512,512]{1,0:T(8,128)(2,1)} %param.7) | copy-start | bytes 1572868
  6.5 155.2 %all-gather.3.cloned.1.call-start = ((), (), s32[]{:S(2)}) async-start(), calls=%async_computation.1 | async-start | bytes 8454144 | tf_op jit(solution)/shard_map/all_gather | solution.py:80
  9.6 21.1 %collective-permute-start.2 = (bf16[2,128,128]{2,0,1:T(2,128)(2,1)S(1)}, bf16[2,128,128]{2,0,1:T(2,128)(2,1)S(1)}, u32[]{:S(2)}, u32[]{:S(2)}) collective-permute-start(bf16[2,128,128]{2,0,1:T(2,128)(2,1)S(1)} %fusion.76), channel_id=1, source_target_pairs={{0,4},{4,8},{8,12},{12,16},{16,20},{20,24},{24,28},{28,32},{32,36}... | collective-permute-start | bytes 196616 | tf_op jit(solution)/shard_map/ppermute | solution.py:19
  11.6 19.1 %collective-permute-start.3 = (bf16[2,128,128]{2,0,1:T(2,128)(2,1)S(1)}, bf16[2,128,128]{2,0,1:T(2,128)(2,1)S(1)}, u32[]{:S(2)}, u32[]{:S(2)}) collective-permute-start(bf16[2,128,128]{2,0,1:T(2,128)(2,1)S(1)} %fusion.76), channel_id=1, source_target_pairs={{4,0},{8,4},{12,8},{16,12},{20,16},{24,20},{28,24},{32,28},{36,32}... | collective-permute-start | bytes 196616 | tf_op jit(solution)/shard_map/ppermute | solution.py:21
  19.5 13.4 %collective-permute-start = (bf16[2,128,128]{2,0,1:T(2,128)(2,1)S(1)}, bf16[2,128,128]{2,0,1:T(2,128)(2,1)S(1)}, u32[]{:S(2)}, u32[]{:S(2)}) collective-permute-start(bf16[2,128,128]{2,0,1:T(2,128)(2,1)S(1)} %get-tuple-element.45), channel_id=1, source_target_pairs={{0,4},{4,8},{8,12},{12,16},{16,20},{20,24},{24,28},{28,32},{32,36}... | collective-permute-start | bytes 196616 | tf_op jit(solution)/shard_map/ppermute | solution.py:19
  21.4 11.5 %collective-permute-start.1 = (bf16[2,128,128]{2,0,1:T(2,128)(2,1)S(1)}, bf16[2,128,128]{2,0,1:T(2,128)(2,1)S(1)}, u32[]{:S(2)}, u32[]{:S(2)}) collective-permute-start(bf16[2,128,128]{2,0,1:T(2,128)(2,1)S(1)} %get-tuple-element.46), channel_id=1, source_target_pairs={{4,0},{8,4},{12,8},{16,12},{20,16},{24,20},{28,24},{32,28},{36,32}... | collective-permute-start | bytes 196616 | tf_op jit(solution)/shard_map/ppermute | solution.py:21
  32.0 3.3 copy-start.9
  35.2 1.2 copy-start.5
  328.9 2.2 copy-start.1
  331.2 1.2 copy-start.2
  331.3 1.4 copy-start.7
  331.3 1.4 copy-start.8
  332.5 1.1 copy-start.4
  332.6 1.2 copy-start.6
  333.3 1.3 copy-start.3
Sparse Core Ops, SparseCore 0:
  10.5 151.2 all-gather.2
where the time goes:
time: 357 us; the launch traced here: 354 us
  local copies, waits for them, and re-layouts  161 us (45%)
  waiting for transfers between devices  124 us (35%)
  other arithmetic  24 us (7%)
  starting transfers between devices  15.3 us (4%)
  between operations  14 us (4%)
  blocking collectives  9.71 us (3%)
  matrix products  5.36 us (2%)
    all_gather x1, waiting for transfers between devices, shards(): everything = lax.all_gather(own_block, 'seq', axis=1, tiled=True)  124 us
    unnamed x54, local copies, waits for them, and re-layouts  90 us
    slice x6, local copies, waits for them, and re-layouts, average_pairs(): return (0.5 * (widened[:, :, 0] + widened[:, :, 1])).astype(jnp.bfloat16)  43.9 us
    convert_element_type x8, other arithmetic, average_pairs(): return (0.5 * (widened[:, :, 0] + widened[:, :, 1])).astype(jnp.bfloat16)  21.3 us
    convert_element_type x5, local copies, waits for them, and re-layouts, average_pairs(): stacked.astype(jnp.float32)  14.7 us
    ppermute x2, starting transfers between devices, extended_2(): lax.ppermute(head, axis, [((i + 1) % count, i) for i in range(ends)])  11.5 us
    all_to_all x1, blocking collectives, shards(): lax.all_to_all(as_sent(attended), 'head', split_axis=0, concat_axis=1, ti...  9.71 us
  transfers between devices with their start and end apart: 5, of which 1 were waited for; matrix products, arithmetic and copies ran while one was open for 4% of the time, Pallas kernels for 0%

commit v1 on v0

--- a/solution.py
+++ b/solution.py
@@ -152,8 +152,11 @@
         return jnp.concatenate(head_outputs, axis=-1).reshape(leaves_step * LEAF, width)
 
     attended = lax.map(attend, jnp.arange(step_count, dtype=jnp.int32)).reshape(tok_count, width)
-    gathered_rows = lax.all_to_all(
-        as_sent(attended), "head", split_axis=0, concat_axis=1, tiled=True
+    gathered_rows = jnp.concatenate(
+        lax.all_to_all(
+            jnp.stack(jnp.split(as_sent(attended), lax.axis_size("head"), axis=0)), "head", 0, 0
+        ),
+        axis=1,
     ).astype(attended.dtype)
     return jnp.dot(gathered_rows, out_weight, preferred_element_type=jnp.float32).astype(
         jnp.bfloat16

time: 357 us -> 357 us (level)
  no operation moved by 1% of the time
where the time goes in v1:
time: 357 us; the launch traced here: 354 us
  local copies, waits for them, and re-layouts  162 us (45%)
  waiting for transfers between devices  124 us (35%)
  other arithmetic  24.1 us (7%)
  starting transfers between devices  15.3 us (4%)
  between operations  14 us (4%)
  blocking collectives  9.72 us (3%)
  matrix products  5.34 us (1%)
    all_gather x1, waiting for transfers between devices, shards(): everything = lax.all_gather(own_block, 'seq', axis=1, tiled=True)  124 us
    unnamed x54, local copies, waits for them, and re-layouts  90.1 us
    slice x6, local copies, waits for them, and re-layouts, average_pairs(): return (0.5 * (widened[:, :, 0] + widened[:, :, 1])).astype(jnp.bfloat16)  43.9 us
    convert_element_type x8, other arithmetic, average_pairs(): return (0.5 * (widened[:, :, 0] + widened[:, :, 1])).astype(jnp.bfloat16)  21.3 us
    convert_element_type x5, local copies, waits for them, and re-layouts, average_pairs(): stacked.astype(jnp.float32)  14.7 us
    ppermute x2, starting transfers between devices, extended_2(): lax.ppermute(head, axis, [((i + 1) % count, i) for i in range(ends)])  11.5 us
    all_to_all x1, blocking collectives, shards(): lax.all_to_all(jnp.stack(jnp.split(as_sent(attended), lax.axis_size('head...  9.72 us
  transfers between devices with their start and end apart: 5, of which 1 were waited for; matrix products, arithmetic and copies ran while one was open for 4% of the time, Pallas kernels for 0%

profile of v1, /device:TPU:32, one launch (start us, length us, event | category | flops | bytes accessed | tf_op | source)
XLA Modules:
  0.0 354.2 jit_solution(13869838341721586421)
XLA Ops:
  6.5 1.0 copy.43
  7.5 0.9 copy.44
  9.6 1.9 collective-permute-start.2
  11.6 5.8 %collective-permute-start.3 = (bf16[2,128,128]{2,0,1:T(2,128)(2,1)S(1)}, bf16[2,128,128]{2,0,1:T(2,128)(2,1)S(1)}, u32[]{:S(2)}, u32[]{:S(2)}) collective-permute-start(bf16[2,128,128]{2,0,1:T(2,128)(2,1)S(1)} %fusion.76), channel_id=1, source_target_pairs={{4,0},{8,4},{12,8},{16,12},{20,16},{24,20},{28,24},{32,28},{36,32}... | collective-permute-start | bytes 196616 | tf_op jit(solution)/shard_map/ppermute | solution.py:21
  17.3 0.9 copy.41
  18.3 0.9 copy.42
  19.5 1.9 collective-permute-start
  21.4 5.8 %collective-permute-start.1 = (bf16[2,128,128]{2,0,1:T(2,128)(2,1)S(1)}, bf16[2,128,128]{2,0,1:T(2,128)(2,1)S(1)}, u32[]{:S(2)}, u32[]{:S(2)}) collective-permute-start(bf16[2,128,128]{2,0,1:T(2,128)(2,1)S(1)} %get-tuple-element.46), channel_id=1, source_target_pairs={{4,0},{8,4},{12,8},{16,12},{20,16},{24,20},{28,24},{32,28},{36,32}... | collective-permute-start | bytes 196616 | tf_op jit(solution)/shard_map/ppermute | solution.py:21
  31.0 0.8 gather_fusion.1
  32.0 0.8 gather_fusion.2
  33.4 1.3 gather_fusion
  35.2 1.2 fusion.70
  36.4 1.2 fusion.68
  37.7 124.1 %all-gather.3.cloned.1.call-done = bf16[2,16384,1,128]{3,0,2,1:T(2,128)(2,1)} async-done(((bf16[2,128,1,128]{3,0,2,1:T(2,128)(2,1)}), bf16[2,16384,1,128]{3,0,2,1:T(2,128)(2,1)}) %all-gather.3.cloned.1.call-update) | async-done | bytes 8388624 | tf_op jit(solution)/shard_map/all_gather | solution.py:80
  161.8 5.1 %copy.50 = bf16[2,16384,1,128]{3,1,0,2:T(8,128)(2,1)S(1)} copy(bf16[2,16384,1,128]{3,0,2,1:T(2,128)(2,1)} %all-gather.3.cloned.1.call-done) | data formatting | bytes 16777216 | tf_op jit(solution)/shard_map/all_gather | solution.py:80
  166.8 13.0 %fusion.63 = (f32[2,8192,1,128]{3,2,1,0:T(1,128)}, f32[2,8192,1,128]{3,2,1,0:T(1,128)}) fusion(bf16[2,8192,2,128]{3,2,1,0:T(2,128)(2,1)S(1)} %bitcast.105), kind=kLoop, calls=%fused_computation.151 | loop fusion | bytes 33554432 | tf_op jit(solution)/shard_map/slice | solution.py:38
  179.8 18.0 %copy.76 = f32[2,8192,1,128]{1,3,0,2:T(8,128)} copy(f32[2,8192,1,128]{3,2,1,0:T(1,128)} %get-tuple-element.22) | data formatting | bytes 16777216
  197.9 18.1 %copy.77 = f32[2,8192,1,128]{1,3,0,2:T(8,128)} copy(f32[2,8192,1,128]{3,2,1,0:T(1,128)} %get-tuple-element.21) | data formatting | bytes 16777216
  215.9 9.4 %multiply_convert_fusion = bf16[2,8192,1,128]{1,3,0,2:T(8,128)(2,1)} fusion(f32[2,8192,1,128]{1,3,0,2:T(8,128)} %copy.76, f32[2,8192,1,128]{1,3,0,2:T(8,128)} %copy.77), kind=kLoop, calls=%fused_computation.3 | loop fusion | flops 6291456 | bytes 20971520 | tf_op jit(solution)/shard_map/convert_element_type | solution.py:38
  225.3 7.0 %copy.53 = f32[2,8192,1,128]{3,1,0,2:T(8,128)} copy(bf16[2,8192,1,128]{1,3,0,2:T(8,128)(2,1)} %multiply_convert_fusion) | data formatting | bytes 12582912 | tf_op jit(solution)/shard_map/convert_element_type | solution.py:37
  232.4 11.5 %fusion.62 = (f32[2,4096,1,128]{3,2,1,0:T(1,128)}, f32[2,4096,1,128]{3,2,1,0:T(1,128)}) fusion(f32[2,4096,2,128]{3,2,1,0:T(2,128)} %bitcast.110), kind=kLoop, calls=%fused_computation.150 | loop fusion | bytes 16777216 | tf_op jit(solution)/shard_map/slice | solution.py:38
  243.9 10.2 %copy.78 = f32[2,4096,1,128]{1,3,0,2:T(8,128)} copy(f32[2,4096,1,128]{3,2,1,0:T(1,128)} %get-tuple-element.20) | data formatting | bytes 8388608
  254.1 10.1 %copy.79 = f32[2,4096,1,128]{1,3,0,2:T(8,128)} copy(f32[2,4096,1,128]{3,2,1,0:T(1,128)} %get-tuple-element.19) | data formatting | bytes 8388608
  264.2 4.3 %multiply_convert_fusion.1 = bf16[2,4096,1,128]{1,3,0,2:T(8,128)(2,1)S(1)} fusion(f32[2,4096,1,128]{1,3,0,2:T(8,128)} %copy.78, f32[2,4096,1,128]{1,3,0,2:T(8,128)} %copy.79), kind=kLoop, calls=%fused_computation.4 | loop fusion | flops 3145728 | bytes 10485760 | tf_op jit(solution)/shard_map/convert_element_type | solution.py:38
  268.6 2.9 copy.56
  271.5 8.0 %fusion.64 = (f32[2,2048,1,128]{3,2,1,0:T(1,128)}, f32[2,2048,1,128]{3,2,1,0:T(1,128)}) fusion(f32[2,2048,2,128]{3,2,1,0:T(2,128)} %bitcast.113), kind=kLoop, calls=%fused_computation.152 | loop fusion | bytes 8388608 | tf_op jit(solution)/shard_map/slice | solution.py:38
  279.5 6.1 %copy.80 = f32[2,2048,1,128]{1,3,0,2:T(8,128)} copy(f32[2,2048,1,128]{3,2,1,0:T(1,128)} %get-tuple-element.32) | data formatting | bytes 4194304
  285.6 6.0 %copy.81 = f32[2,2048,1,128]{1,3,0,2:T(8,128)} copy(f32[2,2048,1,128]{3,2,1,0:T(1,128)} %get-tuple-element.23) | data formatting | bytes 4194304
  291.6 3.6 %multiply_convert_fusion.2 = bf16[2,2048,1,128]{1,3,0,2:T(8,128)(2,1)} fusion(f32[2,2048,1,128]{1,3,0,2:T(8,128)} %copy.80, f32[2,2048,1,128]{1,3,0,2:T(8,128)} %copy.81), kind=kLoop, calls=%fused_computation.11 | loop fusion | flops 1572864 | bytes 5242880 | tf_op jit(solution)/shard_map/convert_element_type | solution.py:38
  295.3 2.6 copy.59
  297.8 5.4 %fusion.65 = (f32[2,1024,1,128]{3,2,1,0:T(1,128)}, f32[2,1024,1,128]{3,2,1,0:T(1,128)}) fusion(f32[2,1024,2,128]{3,2,1,0:T(2,128)} %bitcast.116), kind=kLoop, calls=%fused_computation.153 | loop fusion | bytes 4194304 | tf_op jit(solution)/shard_map/slice | solution.py:38
  303.3 3.6 %copy.82 = f32[2,1024,1,128]{1,3,0,2:T(8,128)} copy(f32[2,1024,1,128]{3,2,1,0:T(1,128)} %get-tuple-element.36) | data formatting | bytes 2097152
  306.9 3.6 %copy.83 = f32[2,1024,1,128]{1,3,0,2:T(8,128)} copy(f32[2,1024,1,128]{3,2,1,0:T(1,128)} %get-tuple-element.34) | data formatting | bytes 2097152
  310.5 1.8 multiply_convert_fusion.3
  312.3 1.2 copy.62
  313.5 3.5 fusion.66
  317.0 1.9 copy.84
  318.9 1.9 copy.85
  320.8 1.3 multiply_convert_fusion.4
  322.1 0.9 copy.65
  323.1 2.5 fusion.67
  325.5 1.8 copy.86
  327.3 1.8 copy.87
  329.1 1.0 fusion.27
  330.1 1.2 copy-done.1
  331.5 1.1 copy-done.2
  336.8 9.7 %all_to_all.5 = bf16[4,64,128]{2,1,0:T(8,128)(2,1)S(1)} all-to-all(bf16[4,64,128]{2,1,0:T(8,128)(2,1)S(1)} %pad_maximum_fusion.5), channel_id=1, replica_groups=mesh['seq'=128,'head'=4] {'head'}, dimensions={0} | all-to-all | bytes 131072 | tf_op jit(solution)/shard_map/all_to_all | solution.py:156
  346.6 0.8 convolution_convert_fusion
  (103 shorter events, 10.4 us)
Async XLA Ops:
  6.5 340.0 %copy-start = (bf16[512,512]{1,0:T(8,128)(2,1)S(1)}, bf16[512,512]{1,0:T(8,128)(2,1)}, u32[]{:S(2)}) copy-start(bf16[512,512]{1,0:T(8,128)(2,1)} %param.7) | copy-start | bytes 1572868
  6.5 155.2 %all-gather.3.cloned.1.call-start = ((), (), s32[]{:S(2)}) async-start(), calls=%async_computation.1 | async-start | bytes 8454144 | tf_op jit(solution)/shard_map/all_gather | solution.py:80
  9.6 21.1 %collective-permute-start.2 = (bf16[2,128,128]{2,0,1:T(2,128)(2,1)S(1)}, bf16[2,128,128]{2,0,1:T(2,128)(2,1)S(1)}, u32[]{:S(2)}, u32[]{:S(2)}) collective-permute-start(bf16[2,128,128]{2,0,1:T(2,128)(2,1)S(1)} %fusion.76), channel_id=1, source_target_pairs={{0,4},{4,8},{8,12},{12,16},{16,20},{20,24},{24,28},{28,32},{32,36}... | collective-permute-start | bytes 196616 | tf_op jit(solution)/shard_map/ppermute | solution.py:19
  11.6 19.1 %collective-permute-start.3 = (bf16[2,128,128]{2,0,1:T(2,128)(2,1)S(1)}, bf16[2,128,128]{2,0,1:T(2,128)(2,1)S(1)}, u32[]{:S(2)}, u32[]{:S(2)}) collective-permute-start(bf16[2,128,128]{2,0,1:T(2,128)(2,1)S(1)} %fusion.76), channel_id=1, source_target_pairs={{4,0},{8,4},{12,8},{16,12},{20,16},{24,20},{28,24},{32,28},{36,32}... | collective-permute-start | bytes 196616 | tf_op jit(solution)/shard_map/ppermute | solution.py:21
  19.5 13.4 %collective-permute-start = (bf16[2,128,128]{2,0,1:T(2,128)(2,1)S(1)}, bf16[2,128,128]{2,0,1:T(2,128)(2,1)S(1)}, u32[]{:S(2)}, u32[]{:S(2)}) collective-permute-start(bf16[2,128,128]{2,0,1:T(2,128)(2,1)S(1)} %get-tuple-element.45), channel_id=1, source_target_pairs={{0,4},{4,8},{8,12},{12,16},{16,20},{20,24},{24,28},{28,32},{32,36}... | collective-permute-start | bytes 196616 | tf_op jit(solution)/shard_map/ppermute | solution.py:19
  21.4 11.5 %collective-permute-start.1 = (bf16[2,128,128]{2,0,1:T(2,128)(2,1)S(1)}, bf16[2,128,128]{2,0,1:T(2,128)(2,1)S(1)}, u32[]{:S(2)}, u32[]{:S(2)}) collective-permute-start(bf16[2,128,128]{2,0,1:T(2,128)(2,1)S(1)} %get-tuple-element.46), channel_id=1, source_target_pairs={{4,0},{8,4},{12,8},{16,12},{20,16},{24,20},{28,24},{32,28},{36,32}... | collective-permute-start | bytes 196616 | tf_op jit(solution)/shard_map/ppermute | solution.py:21
  32.0 3.3 copy-start.9
  35.2 1.2 copy-start.5
  329.1 2.2 copy-start.1
  331.4 1.2 copy-start.2
  331.5 1.4 copy-start.7
  331.5 1.4 copy-start.8
  332.7 1.1 copy-start.4
  332.8 1.2 copy-start.6
  333.5 1.3 copy-start.3
Sparse Core Ops, SparseCore 0:
  10.5 151.2 all-gather.2
